TPU v7x, 512 devices: a whole 4x8x8 slice. The times are simulated.
512 devices in a mesh: leaf: 64 (over z_lo, x, y), head: 8 (over z_hi, core).
Axes of the slice: x: 4, y: 8, z: 8 (z_hi: 4, z_lo: 2; z = z_hi * 2 + z_lo), core: 2. Of those that a mesh axis runs over, the one named last changes fastest.
Arguments:
- queries: bfloat16 [8192, 64, 576], P('leaf', 'head'), may hold values from -40 to 40
- leaf_latent: bfloat16 [8192, 576], P('leaf'), may hold values from -4 to 4
- node_latent: bfloat16 [64, 96, 576], P('leaf', 'head'), may hold values from -4 to 4
- grad_out: bfloat16 [8192, 64, 512], P('leaf', 'head'), may hold values from -6 to 6
- leaf_nodes: int32 [128, 3], P('leaf'), may hold values from 0 to 63, as said below
- leaf_lengths: int32 [128], P('leaf'), may hold values from 1 to 64, 5120 in all
Outputs:
- attention: bfloat16 [8192, 64, 512], P('leaf', 'head')
- node_grad: bfloat16 [64, 96, 576], P('leaf', 'head')
- leaf_grad: bfloat16 [8192, 576], P('leaf')
Inputs may be any that keep to these rules, and one draw needn't show every extreme that they name: `leaf_nodes`: each row lists three different nodes: a root, one of its children and one of that child's children. Every node has one level and one parent; which nodes are used and how often varies.
All inputs are finite; a program needn't handle non-finite values. No bound on the sum of `leaf_lengths` on one device may be relied on, other than what follows from the above.
Results may differ from a plain program's by a relative error of at most 0.0095.
Values may be sent and summed in bfloat16 or wider, within the bound.
A program may use at most 64 MiB of HBM per device.

v0:
```python
import jax
import jax.numpy as jnp
from jax import lax
from jax.sharding import PartitionSpec as P

LAT = 512
NODE_ROWS = 96
score_scale = 192.0 ** (-0.5)


def from_everyone(shard, axis):
    devices = lax.axis_size(axis)
    return lax.all_to_all(
        jnp.broadcast_to(shard[None], (devices, *shard.shape)), axis, 0, 0, tiled=True
    )


def in_order(pieces, dim):
    pieces = jnp.moveaxis(pieces, 0, dim)
    lengths = pieces.shape
    return pieces.reshape(*lengths[:dim], lengths[dim] * lengths[dim + 1], *lengths[dim + 2 :])


def gather_directly(shard, axis, dim):
    pieces = from_everyone(shard, axis)
    return in_order(pieces, dim)


def cut_along(shard, dim, devices):
    before, after = (shard.shape[:dim], shard.shape[dim + 1 :])
    return jnp.moveaxis(shard.reshape(*before, devices, -1, *after), dim, 0)


def sum_at_owner(shard, axis, dim):
    pieces = cut_along(shard, dim, lax.axis_size(axis))
    arrived = lax.all_to_all(pieces, axis, split_axis=0, concat_axis=0, tiled=True)
    return arrived.astype(jnp.float32).sum(axis=0)


def body(queries, leaf_latent, node_latent, grad_out, leaf_nodes, leaf_lengths):
    rows, heads, width = queries.shape
    leaves = leaf_nodes.shape[0]
    leaf_rows = rows // leaves
    slices = gather_directly(node_latent, "leaf", 0)
    total_nodes = slices.shape[0]
    node_ids = leaf_nodes.reshape(-1)
    picker = (node_ids[:, None] == jnp.arange(total_nodes, dtype=jnp.int32)[None, :]).astype(
        jnp.bfloat16
    )
    chosen = jnp.dot(picker, slices.reshape(total_nodes, -1), preferred_element_type=jnp.float32)
    chosen = chosen.astype(jnp.bfloat16).reshape(leaves * 3, -1, width)
    whole_nodes = gather_directly(chosen, "head", 1)
    node_keys = whole_nodes.reshape(leaves, 3 * NODE_ROWS, width)
    keys = jnp.concatenate([node_keys, leaf_latent.reshape(leaves, leaf_rows, width)], axis=1)
    values = keys[:, :, :LAT]
    total_keys = keys.shape[1]
    query = queries.reshape(leaves, leaf_rows * heads, width)
    row_of = jnp.arange(leaf_rows * heads, dtype=jnp.int32) // heads
    key_index = jnp.arange(total_keys, dtype=jnp.int32)
    visible = (key_index[None, :] < 3 * NODE_ROWS) | (
        key_index[None, :] - 3 * NODE_ROWS <= row_of[:, None]
    )
    live = (row_of[None, :] < leaf_lengths[:, None]).astype(jnp.float32)[..., None]
    scores = (
        jnp.einsum("lqc,lkc->lqk", query, keys, preferred_element_type=jnp.float32) * score_scale
    )
    scores = jnp.where(visible[None], scores, -jnp.inf)
    top = jnp.max(scores, axis=-1, keepdims=True)
    expo = jnp.exp(scores - top)
    probs = expo / jnp.sum(expo, axis=-1, keepdims=True)
    probs_b = probs.astype(jnp.bfloat16)
    outputs = jnp.einsum("lqk,lkc->lqc", probs_b, values, preferred_element_type=jnp.float32)
    attention = (outputs * live).astype(jnp.bfloat16).reshape(rows, heads, LAT)
    masked_f = grad_out.reshape(leaves, leaf_rows * heads, LAT).astype(jnp.float32) * live
    masked = masked_f.astype(jnp.bfloat16)
    dprobs = jnp.einsum("lqc,lkc->lqk", masked, values, preferred_element_type=jnp.float32)
    delta = jnp.sum(masked_f * outputs, axis=-1)
    dscores = (score_scale * probs * (dprobs - delta[..., None])).astype(jnp.bfloat16)
    grad_keys = jnp.einsum("lqk,lqc->lkc", dscores, query, preferred_element_type=jnp.float32)
    grad_values = jnp.einsum("lqk,lqc->lkc", probs_b, masked, preferred_element_type=jnp.float32)
    grad_keys = jnp.concatenate(
        [grad_keys[:, :, :LAT] + grad_values, grad_keys[:, :, LAT:]], axis=2
    )
    node_terms = grad_keys[:, : 3 * NODE_ROWS].reshape(leaves * 3, NODE_ROWS, width)
    own_terms = grad_keys[:, 3 * NODE_ROWS :].reshape(rows, width)
    head_shares = sum_at_owner(node_terms.astype(jnp.bfloat16), "head", 1)
    owned = node_latent.shape[0]
    spread = jnp.dot(
        picker.T.astype(jnp.float32),
        head_shares.reshape(leaves * 3, -1),
        precision=lax.Precision.HIGHEST,
    )
    arrived = lax.all_to_all(
        spread.astype(jnp.bfloat16), "leaf", split_axis=0, concat_axis=0, tiled=True
    ).astype(spread.dtype)
    mine = jnp.sum(arrived.reshape(-1, owned, arrived.shape[1]), axis=0)
    node_grad = mine.reshape(node_latent.shape).astype(jnp.bfloat16)
    leaf_grad = lax.psum(own_terms, "head").astype(jnp.bfloat16)
    return (attention, node_grad, leaf_grad)


def solution(mesh):
    return jax.shard_map(
        body,
        mesh=mesh,
        in_specs=(
            P("leaf", "head", None),
            P("leaf", None),
            P("leaf", "head", None),
            P("leaf", "head", None),
            P("leaf", None),
            P("leaf"),
        ),
        out_specs=(P("leaf", "head", None), P("leaf", "head", None), P("leaf", None)),
        check_vma=False,
    )
```

profile of v0, /device:TPU:10, one launch (start us, length us, event | category | flops | bytes accessed | tf_op | source)
XLA Modules:
  0.0 189.7 jit_solution(587049199212427704)
XLA Ops:
  0.6 1.9 broadcast_in_dim.18
  2.5 12.5 %all-to-all-start = ((bf16[64,1,12,576]{3,2,1,0:T(8,128)(2,1)}), bf16[64,1,12,576]{3,2,1,0:T(8,128)(2,1)S(1)}, u32[]{:S(2)}, u32[]{:S(2)}) async-start(bf16[64,1,12,576]{3,2,1,0:T(8,128)(2,1)} %broadcast_in_dim.18), calls=%async_computation | async-start | bytes 2621440 | tf_op jit(solution)/shard_map/all_to_all | solution.py:13
  15.1 34.0 %all-to-all-done = bf16[64,1,12,576]{3,2,1,0:T(8,128)(2,1)S(1)} async-done(((bf16[64,1,12,576]{3,2,1,0:T(8,128)(2,1)}), bf16[64,1,12,576]{3,2,1,0:T(8,128)(2,1)S(1)}, u32[]{:S(2)}, u32[]{:S(2)}) %all-to-all-start) | async-done | bytes 884768 | tf_op jit(solution)/shard_map/all_to_all | solution.py:13
  49.1 0.9 reshape_reshape.6
  50.5 1.0 broadcast_in_dim.24
  51.5 9.5 %all-to-all-start.1 = ((bf16[8,6,12,576]{3,2,1,0:T(8,128)(2,1)}), bf16[8,6,12,576]{3,2,1,0:T(8,128)(2,1)S(1)}, u32[]{:S(2)}, u32[]{:S(2)}) async-start(bf16[8,6,12,576]{3,2,1,0:T(8,128)(2,1)} %broadcast_in_dim.24), calls=%async_computation.1 | async-start | bytes 1966080 | tf_op jit(solution)/shard_map/all_to_all | solution.py:13
  61.2 0.9 copy.25
  62.1 2.0 %copy.26 = bf16[128,8,576]{2,1,0:T(8,128)(2,1)} copy(bf16[128,8,576]{0,2,1:T(8,128)(2,1)S(1)} %copy-done.1) | data formatting | bytes 2359296 | tf_op args[0]
  65.1 24.2 %all-to-all-done.1 = bf16[8,6,12,576]{3,2,1,0:T(8,128)(2,1)S(1)} async-done(((bf16[8,6,12,576]{3,2,1,0:T(8,128)(2,1)}), bf16[8,6,12,576]{3,2,1,0:T(8,128)(2,1)S(1)}, u32[]{:S(2)}, u32[]{:S(2)}) %all-to-all-start.1) | async-done | bytes 663584 | tf_op jit(solution)/shard_map/all_to_all | solution.py:13
  89.7 1.2 copy.24
  91.3 2.5 %fusion.9 = f32[2,512,352]{1,2,0:T(8,128)S(1)} fusion(bf16[2,512,576]{2,1,0:T(8,128)(2,1)S(1)} %bitcast.30, bf16[2,64,576]{1,2,0:T(8,128)(2,1)} %copy.25, bf16[2,288,576]{1,2,0:T(8,128)(2,1)} %copy.24, pred[512,352]{0,1:T(8,128)(4,1)} %compare_or_fusion), kind=kOutput, calls=%fused_computation.18 | convolution fusion | flops 417579008 | bytes 3612672 | tf_op jit(solution)/shard_map/lqc,lkc->lqk/dot_general | solution.py:65
  93.7 1.4 fusion.31
  95.1 2.2 %fusion.18 = f32[2,512,512]{2,1,0:T(8,128)S(1)} fusion(bf16[2,64,576]{1,2,0:T(8,128)(2,1)} %copy.25, bf16[2,288,576]{1,2,0:T(8,128)(2,1)} %copy.24, f32[2,512]{1,0:T(2,128)S(1)} %get-tuple-element.12, f32[2,512,352]{1,2,0:T(8,128)S(1)} %fusion.9), kind=kOutput, calls=%fused_computation.31 | convolution fusion | flops 371623264 | bytes 4354048 | tf_op jit(solution)/shard_map/lqk,lkc->lqc/dot_general | solution.py:72
  97.3 3.0 %fusion.4 = (f32[2,512]{1,0:T(2,128)S(1)}, bf16[2,512,512]{2,1,0:T(8,128)(2,1)}, bf16[2,512,512]{2,1,0:T(8,128)(2,1)}) fusion(f32[2,512,512]{2,1,0:T(8,128)S(1)} %fusion.18, f32[2,512]{1,0:T(2,128)S(1)} %compare_convert_fusion, bf16[2,512,512]{2,1,0:T(8,128)(2,1)} %bitcast.32), kind=kLoop, calls=%fused_computation.7 | loop fusion | flops 3668992 | bytes 5251072 | tf_op jit(solution)/shard_map/reduce_sum | solution.py:77
  100.4 5.2 %fusion.11 = f32[2,352,576]{1,2,0:T(8,128)} fusion(bf16[2,512,576]{2,1,0:T(8,128)(2,1)} %bitcast.29, bf16[2,512,512]{2,1,0:T(8,128)(2,1)} %get-tuple-element.11, f32[2,512]{1,0:T(2,128)S(1)} %get-tuple-element.9, f32[2,512,352]{1,2,0:T(8,128)} %get-tuple-element.13, f32[2,512]{1,0:T(2,128)S(1)} %get-tuple-element.12, bf16[2,64,576]{1,2,0:T(8,128)(2,1)} %copy.25, ...), kind=kOutput, calls=%fused_computation.20 | convolution fusion | flops 787578880 | bytes 6111232 | tf_op jit(solution)/shard_map/lqk,lqc->lkc/dot_general | solution.py:79
  105.5 2.5 %slice_add_fusion = f32[2,352,512]{1,2,0:T(8,128)S(1)} fusion(f32[2,352,576]{1,2,0:T(8,128)} %fusion.11, bf16[2,512,512]{2,1,0:T(8,128)(2,1)} %get-tuple-element.11, f32[2,512]{1,0:T(2,128)S(1)} %get-tuple-element.12, f32[2,512,352]{1,2,0:T(8,128)S(1)} %fusion.9), kind=kOutput, calls=%fused_computation.12 | convolution fusion | flops 370541920 | bytes 6819840 | tf_op jit(solution)/shard_map/lqk,lqc->lkc/dot_general | solution.py:80
  108.1 0.9 slice.22
  110.0 30.0 %all_to_all.24 = bf16[8,6,12,576]{3,2,1,0:T(8,128)(2,1)S(1)} all-to-all(bf16[8,6,12,576]{3,2,1,0:T(8,128)(2,1)S(1)} %copy.33), channel_id=1, replica_groups=mesh['leaf'=64,'head'=8] {'head'}, dimensions={0} | all-to-all | bytes 1327104 | tf_op jit(solution)/shard_map/all_to_all | solution.py:36
  140.3 1.0 fusion.1
  141.8 1.3 reduce.2
  143.1 1.2 reshape.168
  144.2 6.5 %all-to-all-start.3 = ((bf16[64,2,3456]{2,1,0:T(2,128)(2,1)}), bf16[64,2,3456]{2,1,0:T(2,128)(2,1)S(1)}, u32[]{:S(2)}, u32[]{:S(2)}) async-start(bf16[64,2,3456]{2,1,0:T(2,128)(2,1)} %reshape.168), calls=%async_computation.3 | async-start | bytes 1769472 | tf_op jit(solution)/shard_map/all_to_all | solution.py:93
  151.2 34.6 %all-reduce.1 = bf16[128,576]{1,0:T(8,128)(2,1)S(1)} all-reduce(f32[128,576]{1,0:T(8,128)S(1)} %bitcast.31), channel_id=1, replica_groups=mesh['leaf'=64,'head'=8] {'head'}, use_global_device_ids=true, to_apply=%region_5.6 | all-reduce | flops 73728 | bytes 442368 | tf_op jit(solution)/shard_map/psum | solution.py:98
  187.3 1.7 reduce_sum.42
  (34 shorter events, 6.8 us)
Async XLA Ops:
  2.5 12.5 %copy-start.4 = (s32[2,3]{1,0:T(2,128)S(1)}, s32[2,3]{1,0:T(2,128)}, u32[]{:S(2)}) copy-start(s32[2,3]{1,0:T(2,128)} %param.10) | copy-start | bytes 76
  2.5 46.6 %all-to-all-start = ((bf16[64,1,12,576]{3,2,1,0:T(8,128)(2,1)}), bf16[64,1,12,576]{3,2,1,0:T(8,128)(2,1)S(1)}, u32[]{:S(2)}, u32[]{:S(2)}) async-start(bf16[64,1,12,576]{3,2,1,0:T(8,128)(2,1)} %broadcast_in_dim.18), calls=%async_computation | async-start | bytes 2621440 | tf_op jit(solution)/shard_map/all_to_all | solution.py:13
  50.5 10.6 %copy-start.2 = (bf16[128,576]{0,1:T(8,128)(2,1)S(1)}, bf16[128,576]{0,1:T(8,128)(2,1)}, u32[]{:S(2)}) copy-start(bf16[128,576]{0,1:T(8,128)(2,1)} %param.7) | copy-start | bytes 442372
  51.5 10.6 %copy-start.1 = (bf16[128,8,576]{0,2,1:T(8,128)(2,1)S(1)}, bf16[128,8,576]{0,2,1:T(8,128)(2,1)}, u32[]{:S(2)}) copy-start(bf16[128,8,576]{0,2,1:T(8,128)(2,1)} %param.6) | copy-start | bytes 3538948
  51.5 37.7 %all-to-all-start.1 = ((bf16[8,6,12,576]{3,2,1,0:T(8,128)(2,1)}), bf16[8,6,12,576]{3,2,1,0:T(8,128)(2,1)S(1)}, u32[]{:S(2)}, u32[]{:S(2)}) async-start(bf16[8,6,12,576]{3,2,1,0:T(8,128)(2,1)} %broadcast_in_dim.24), calls=%async_computation.1 | async-start | bytes 1966080 | tf_op jit(solution)/shard_map/all_to_all | solution.py:13
  61.2 2.9 %copy-start.3 = (s32[2]{0:T(128)S(1)}, s32[2]{0:T(128)}, u32[]{:S(2)}) copy-start(s32[2]{0:T(128)} %param.11) | copy-start | bytes 28
  89.7 1.5 copy-start
  144.2 42.4 %all-to-all-start.3 = ((bf16[64,2,3456]{2,1,0:T(2,128)(2,1)}), bf16[64,2,3456]{2,1,0:T(2,128)(2,1)S(1)}, u32[]{:S(2)}, u32[]{:S(2)}) async-start(bf16[64,2,3456]{2,1,0:T(2,128)(2,1)} %reshape.168), calls=%async_computation.3 | async-start | bytes 1769472 | tf_op jit(solution)/shard_map/all_to_all | solution.py:93
where the time goes:
time: 190 us
  blocking collectives  64.6 us (34%)
  waiting for transfers between devices  58.2 us (31%)
  starting transfers between devices  28.6 us (15%)
  local copies, waits for them, and re-layouts  15.1 us (8%)
  matrix products  13.6 us (7%)
  other arithmetic  8.84 us (5%)
    all_to_all x2, waiting for transfers between devices, from_everyone(): lax.all_to_all(jnp.broadcast_to(shard[None], (devices, *shard.shape)), ax...  58.2 us
    psum x1, blocking collectives, body(): leaf_grad = lax.psum(own_terms, 'head').astype(jnp.bfloat16)  34.6 us
    all_to_all x1, blocking collectives, sum_at_owner(): lax.all_to_all(pieces, axis, split_axis=0, concat_axis=0, tiled=True)  30 us
    all_to_all x2, starting transfers between devices, from_everyone(): lax.all_to_all(jnp.broadcast_to(shard[None], (devices, *shard.shape)), ax...  22 us
    all_to_all x1, starting transfers between devices, body(): lax.all_to_all(spread.astype(jnp.bfloat16), 'leaf', split_axis=0, concat_...  6.53 us
    dot_general x1, matrix products, body(): jnp.einsum('lqk,lqc->lkc', dscores, query, preferred_element_type=jnp.flo...  5.17 us
    unnamed x15, local copies, waits for them, and re-layouts  5.13 us
  transfers between devices with their start and end apart: 3, of which 2 were waited for; matrix products, arithmetic and copies ran while one was open for 3% of the time, Pallas kernels for 0%

commit v1 on v0

--- a/solution.py
+++ b/solution.py
@@ -95,7 +95,7 @@
     ).astype(spread.dtype)
     mine = jnp.sum(arrived.reshape(-1, owned, arrived.shape[1]), axis=0)
     node_grad = mine.reshape(node_latent.shape).astype(jnp.bfloat16)
-    leaf_grad = lax.psum(own_terms, "head").astype(jnp.bfloat16)
+    leaf_grad = jnp.sum(jax.lax.all_gather(own_terms, "head"), 0).astype(jnp.bfloat16)
     return (attention, node_grad, leaf_grad)
 
 

time: 190 us -> 209 us (1.10)
  the two profiles are of different devices: /device:TPU:10 before, /device:TPU:8 now
where the time goes in v1:
time: 209 us; the launch traced here: 208 us
  blocking collectives  73.3 us (35%)
  waiting for transfers between devices  59 us (28%)
  starting transfers between devices  22.1 us (11%)
  local copies, waits for them, and re-layouts  15.2 us (7%)
  between operations  14.2 us (7%)
  matrix products  13.6 us (7%)
  other arithmetic  10.6 us (5%)
    all_to_all x2, waiting for transfers between devices, from_everyone(): lax.all_to_all(jnp.broadcast_to(shard[None], (devices, *shard.shape)), ax...  59 us
    all_to_all x1, blocking collectives, sum_at_owner(): lax.all_to_all(pieces, axis, split_axis=0, concat_axis=0, tiled=True)  44 us
    all_to_all x1, blocking collectives, body(): lax.all_to_all(spread.astype(jnp.bfloat16), 'leaf', split_axis=0, concat_...  29.3 us
    all_to_all x2, starting transfers between devices, from_everyone(): lax.all_to_all(jnp.broadcast_to(shard[None], (devices, *shard.shape)), ax...  22 us
    dot_general x1, matrix products, body(): jnp.einsum('lqk,lqc->lkc', dscores, query, preferred_element_type=jnp.flo...  5.17 us
    unnamed x16, local copies, waits for them, and re-layouts  4.37 us
  transfers between devices with their start and end apart: 3, of which 2 were waited for; matrix products, arithmetic and copies ran while one was open for 5% of the time, Pallas kernels for 0%

profile of v1, /device:TPU:8, one launch (start us, length us, event | category | flops | bytes accessed | tf_op | source)
XLA Modules:
  0.0 208.0 jit_solution(925171569472437312)
XLA Ops:
  7.2 1.9 broadcast_in_dim.18
  9.1 12.5 %all-to-all-start = ((bf16[64,1,12,576]{3,2,1,0:T(8,128)(2,1)}), bf16[64,1,12,576]{3,2,1,0:T(8,128)(2,1)S(1)}, u32[]{:S(2)}, u32[]{:S(2)}) async-start(bf16[64,1,12,576]{3,2,1,0:T(8,128)(2,1)} %broadcast_in_dim.18), calls=%async_computation | async-start | bytes 2621440 | tf_op jit(solution)/shard_map/all_to_all | solution.py:13
  21.7 34.9 %all-to-all-done = bf16[64,1,12,576]{3,2,1,0:T(8,128)(2,1)S(1)} async-done(((bf16[64,1,12,576]{3,2,1,0:T(8,128)(2,1)}), bf16[64,1,12,576]{3,2,1,0:T(8,128)(2,1)S(1)}, u32[]{:S(2)}, u32[]{:S(2)}) %all-to-all-start) | async-done | bytes 884768 | tf_op jit(solution)/shard_map/all_to_all | solution.py:13
  56.5 0.9 reshape_reshape.6
  57.9 1.0 broadcast_in_dim.24
  58.9 9.5 %all-to-all-start.1 = ((bf16[8,6,12,576]{3,2,1,0:T(8,128)(2,1)}), bf16[8,6,12,576]{3,2,1,0:T(8,128)(2,1)S(1)}, u32[]{:S(2)}, u32[]{:S(2)}) async-start(bf16[8,6,12,576]{3,2,1,0:T(8,128)(2,1)} %broadcast_in_dim.24), calls=%async_computation.1 | async-start | bytes 1966080 | tf_op jit(solution)/shard_map/all_to_all | solution.py:13
  68.7 0.9 copy.24
  69.6 2.0 copy.25
  72.5 24.1 %all-to-all-done.1 = bf16[8,6,12,576]{3,2,1,0:T(8,128)(2,1)S(1)} async-done(((bf16[8,6,12,576]{3,2,1,0:T(8,128)(2,1)}), bf16[8,6,12,576]{3,2,1,0:T(8,128)(2,1)S(1)}, u32[]{:S(2)}, u32[]{:S(2)}) %all-to-all-start.1) | async-done | bytes 663584 | tf_op jit(solution)/shard_map/all_to_all | solution.py:13
  97.2 1.2 copy.23
  98.7 2.5 %fusion.9 = f32[2,512,352]{1,2,0:T(8,128)S(1)} fusion(bf16[2,512,576]{2,1,0:T(8,128)(2,1)S(1)} %bitcast.31, bf16[2,64,576]{1,2,0:T(8,128)(2,1)} %copy.24, bf16[2,288,576]{1,2,0:T(8,128)(2,1)} %copy.23, pred[512,352]{0,1:T(8,128)(4,1)} %compare_or_fusion), kind=kOutput, calls=%fused_computation.18 | convolution fusion | flops 417579008 | bytes 3612672 | tf_op jit(solution)/shard_map/lqc,lkc->lqk/dot_general | solution.py:65
  101.1 1.4 fusion.31
  102.5 2.2 %fusion.18 = f32[2,512,512]{2,1,0:T(8,128)S(1)} fusion(bf16[2,64,576]{1,2,0:T(8,128)(2,1)} %copy.24, bf16[2,288,576]{1,2,0:T(8,128)(2,1)} %copy.23, f32[2,512]{1,0:T(2,128)S(1)} %get-tuple-element.9, f32[2,512,352]{1,2,0:T(8,128)S(1)} %fusion.9), kind=kOutput, calls=%fused_computation.31 | convolution fusion | flops 371623264 | bytes 4354048 | tf_op jit(solution)/shard_map/lqk,lkc->lqc/dot_general | solution.py:72
  104.7 3.0 %fusion.4 = (f32[2,512]{1,0:T(2,128)S(1)}, bf16[2,512,512]{2,1,0:T(8,128)(2,1)}, bf16[2,512,512]{2,1,0:T(8,128)(2,1)}) fusion(f32[2,512,512]{2,1,0:T(8,128)S(1)} %fusion.18, f32[2,512]{1,0:T(2,128)S(1)} %compare_convert_fusion, bf16[2,512,512]{2,1,0:T(8,128)(2,1)} %bitcast.32), kind=kLoop, calls=%fused_computation.7 | loop fusion | flops 3668992 | bytes 5251072 | tf_op jit(solution)/shard_map/reduce_sum | solution.py:77
  107.8 5.2 %fusion.11 = f32[2,352,576]{1,2,0:T(8,128)} fusion(bf16[2,512,576]{2,1,0:T(8,128)(2,1)} %bitcast.30, bf16[2,512,512]{2,1,0:T(8,128)(2,1)} %get-tuple-element.8, f32[2,512]{1,0:T(2,128)S(1)} %get-tuple-element.6, f32[2,512,352]{1,2,0:T(8,128)} %get-tuple-element.10, f32[2,512]{1,0:T(2,128)S(1)} %get-tuple-element.9, bf16[2,64,576]{1,2,0:T(8,128)(2,1)} %copy.24, ...), kind=kOutput, calls=%fused_computation.20 | convolution fusion | flops 787578880 | bytes 6111232 | tf_op jit(solution)/shard_map/lqk,lqc->lkc/dot_general | solution.py:79
  112.9 2.5 %slice_add_fusion = f32[2,352,512]{1,2,0:T(8,128)S(1)} fusion(f32[2,352,576]{1,2,0:T(8,128)} %fusion.11, bf16[2,512,512]{2,1,0:T(8,128)(2,1)} %get-tuple-element.8, f32[2,512]{1,0:T(2,128)S(1)} %get-tuple-element.9, f32[2,512,352]{1,2,0:T(8,128)S(1)} %fusion.9), kind=kOutput, calls=%fused_computation.12 | convolution fusion | flops 370541920 | bytes 6819840 | tf_op jit(solution)/shard_map/lqk,lqc->lkc/dot_general | solution.py:80
  115.5 0.9 slice.22
  116.9 0.9 copy.35
  118.7 44.0 %all_to_all.24 = bf16[8,6,12,576]{3,2,1,0:T(8,128)(2,1)S(1)} all-to-all(bf16[8,6,12,576]{3,2,1,0:T(8,128)(2,1)S(1)} %copy.32), channel_id=1, replica_groups=mesh['leaf'=64,'head'=8] {'head'}, dimensions={0} | all-to-all | bytes 1327104 | tf_op jit(solution)/shard_map/all_to_all | solution.py:36
  163.0 1.0 fusion.1
  164.5 1.3 reduce.2
  166.0 29.3 %all_to_all.25 = bf16[64,2,3456]{2,1,0:T(2,128)(2,1)S(1)} all-to-all(bf16[64,2,3456]{2,1,0:T(2,128)(2,1)S(1)} %reshape.164), channel_id=1, replica_groups=mesh['leaf'=64,'head'=8] {'leaf'}, dimensions={0} | all-to-all | bytes 1769472 | tf_op jit(solution)/shard_map/all_to_all | solution.py:93
  196.0 1.7 reduce_sum.51
  198.4 1.8 reduce_sum.52
  (38 shorter events, 7.2 us)
Async XLA Ops:
  9.1 12.5 %copy-start.4 = (s32[2,3]{1,0:T(2,128)S(1)}, s32[2,3]{1,0:T(2,128)}, u32[]{:S(2)}) copy-start(s32[2,3]{1,0:T(2,128)} %param.10) | copy-start | bytes 76
  9.1 47.5 %all-to-all-start = ((bf16[64,1,12,576]{3,2,1,0:T(8,128)(2,1)}), bf16[64,1,12,576]{3,2,1,0:T(8,128)(2,1)S(1)}, u32[]{:S(2)}, u32[]{:S(2)}) async-start(bf16[64,1,12,576]{3,2,1,0:T(8,128)(2,1)} %broadcast_in_dim.18), calls=%async_computation | async-start | bytes 2621440 | tf_op jit(solution)/shard_map/all_to_all | solution.py:13
  57.9 10.6 %copy-start.2 = (bf16[128,576]{0,1:T(8,128)(2,1)S(1)}, bf16[128,576]{0,1:T(8,128)(2,1)}, u32[]{:S(2)}) copy-start(bf16[128,576]{0,1:T(8,128)(2,1)} %param.7) | copy-start | bytes 442372
  58.9 10.6 %copy-start.1 = (bf16[128,8,576]{0,2,1:T(8,128)(2,1)S(1)}, bf16[128,8,576]{0,2,1:T(8,128)(2,1)}, u32[]{:S(2)}) copy-start(bf16[128,8,576]{0,2,1:T(8,128)(2,1)} %param.6) | copy-start | bytes 3538948
  58.9 37.7 %all-to-all-start.1 = ((bf16[8,6,12,576]{3,2,1,0:T(8,128)(2,1)}), bf16[8,6,12,576]{3,2,1,0:T(8,128)(2,1)S(1)}, u32[]{:S(2)}, u32[]{:S(2)}) async-start(bf16[8,6,12,576]{3,2,1,0:T(8,128)(2,1)} %broadcast_in_dim.24), calls=%async_computation.1 | async-start | bytes 1966080 | tf_op jit(solution)/shard_map/all_to_all | solution.py:13
  68.5 129.9 %all-gather.2.cloned.1.call-start = ((), (), s32[]{:S(2)}) async-start(), calls=%async_computation.4 | async-start | bytes 2654208 | tf_op jit(solution)/shard_map/all_gather | solution.py:98
  68.7 2.9 %copy-start.3 = (s32[2]{0:T(128)S(1)}, s32[2]{0:T(128)}, u32[]{:S(2)}) copy-start(s32[2]{0:T(128)} %param.11) | copy-start | bytes 28
  97.1 1.5 copy-start
Sparse Core Ops, SparseCore 0:
  117.9 50.2 all-gather.1
